TPU v7x, 32 devices: a whole 2x2x4 slice. The times are simulated.
32 devices in a mesh: groups: 2 (over y), att: 16 (over z, x, core), exp: 1.
Axes of the slice: x: 2, y: 2, z: 4, core: 2. Of those that a mesh axis runs over, the one named last changes fastest.
Arguments:
- queries: bfloat16 [1024, 4096], P(('groups', 'att'), 'exp'), parts along dimension 0, may hold values from -40 to 40
- key_cache: bfloat16 [1024, 2, 256, 128], P(('groups', 'att'), 'exp'), parts along dimension 0, may hold values from -12 to 12
- value_cache: bfloat16 [1024, 2, 256, 128], P(('groups', 'att'), 'exp'), parts along dimension 0, may hold values from -6 to 6
- new_key: bfloat16 [1024, 256], P(('groups', 'att'), 'exp'), parts along dimension 0, may hold values from -6 to 6
- new_value: bfloat16 [1024, 256], P(('groups', 'att'), 'exp'), parts along dimension 0, may hold values from -6 to 6
- lengths: int32 [1024], P(('groups', 'att')), parts along dimension 0, may hold values from 2 to 256, as said below
- residual: bfloat16 [1024, 4096], P(('groups', 'att'), 'exp'), parts along dimension 0, may hold values from -40 to 40
- norm_gain: bfloat16 [4096], P('exp'), may hold values from 0.099609375 to 1.8984375
- expert_ids: int32 [1024, 8], P(('groups', 'att')), parts along dimension 0, may hold values from 0 to 15, all different within a row; in each aligned block of 32 rows (0 to 31, 32 to 63, ...) at most 32 rows name the same one
- gate_probs: float32 [1024, 8], P(('groups', 'att')), parts along dimension 0, may hold values from 0.1 to 1
- gate_proj: bfloat16 [16, 4096, 768], P('att', None, 'exp'), may hold values from -0.09375 to 0.09375
- up_proj: bfloat16 [16, 4096, 768], P('att', None, 'exp'), may hold values from -0.09375 to 0.09375
- down_proj: bfloat16 [16, 768, 4096], P('att', 'exp'), may hold values from -0.21875 to 0.21875
Outputs:
- layer_out: bfloat16 [1024, 4096], P(('groups', 'att'), 'exp'), parts along dimension 0
There are 2 independent parts, one for each index of `groups`. A program takes and returns all parts, laid end to end along the dimension named above; an argument that names none is the same for every part. Nothing has to cross between parts.
Inputs may be any that keep to these rules, and one draw needn't show every extreme that they name: `lengths`: position 0 and 1 of every row are live; some row of every draw has all 256 slots live. `expert_ids`: the 8 experts of a row differ. Among the rows of one index of att (aligned blocks of 32 rows) no expert is named more than 32 times, a bound that some block reaches.
All inputs are finite; a program needn't handle non-finite values.
Results may differ from a plain program's by a relative error of at most 0.0051.
Values may be sent and summed in bfloat16 or wider, within the bound.
A program may use at most 128 MiB of HBM per device.

v0:
```python
import math

import jax
import jax.numpy as jnp
from jax import lax
from jax.sharding import PartitionSpec as P


def attend(queries, key_cache, value_cache, new_key, new_value, lengths):
    row_count = queries.shape[0]
    groups_kv = key_cache.shape[1]
    head_dim = key_cache.shape[3]
    per_group = queries.shape[1] // (groups_kv * head_dim)
    scaling = 1.0 / math.sqrt(head_dim)
    query_blocks = queries.reshape(row_count, groups_kv, per_group, head_dim)
    cached = (
        jnp.einsum("rghd,rgpd->rghp", query_blocks, key_cache, preferred_element_type=jnp.float32)
        * scaling
    )
    fresh_keys = new_key.reshape(row_count, groups_kv, head_dim)
    own_score = (
        jnp.einsum("rghd,rgd->rgh", query_blocks, fresh_keys, preferred_element_type=jnp.float32)
        * scaling
    )
    position = lax.broadcasted_iota(jnp.int32, cached.shape, 3)
    valid_keys = position < lengths[:, None, None, None]
    cached = jnp.where(valid_keys, cached, -jnp.inf)
    largest = jnp.maximum(jnp.max(cached, axis=3), own_score)
    exp_cached = jnp.exp(cached - largest[..., None])
    own_exp = jnp.exp(own_score - largest)
    denominator = jnp.sum(exp_cached, axis=3) + own_exp
    weights = (exp_cached / denominator[..., None]).astype(jnp.bfloat16)
    own_weight = (own_exp / denominator).astype(jnp.bfloat16)
    fresh_values = new_value.reshape(row_count, groups_kv, head_dim).astype(jnp.float32)
    attended = jnp.einsum(
        "rghp,rgpd->rghd", weights, value_cache, preferred_element_type=jnp.float32
    )
    attended = attended + own_weight.astype(jnp.float32)[..., None] * fresh_values[:, :, None, :]
    return attended.reshape(row_count, per_group * groups_kv * head_dim)


def body(
    queries,
    key_cache,
    value_cache,
    new_key,
    new_value,
    lengths,
    residual,
    norm_gain,
    expert_ids,
    gate_probs,
    gate_proj,
    up_proj,
    down_proj,
):
    attended = attend(queries, key_cache, value_cache, new_key, new_value, lengths)
    hidden = (residual.astype(jnp.float32) + attended).astype(jnp.bfloat16)
    local_rows, top_count = expert_ids.shape
    width_full = down_proj.shape[2]
    owners = lax.axis_size("att")
    local_experts = gate_proj.shape[0]
    experts_all = owners * local_experts
    capacity = min(local_rows, max(2, 2 * local_rows * top_count // experts_all))
    full_rows, full_gain = (
        lax.all_gather(hidden, "exp", axis=1, tiled=True),
        lax.all_gather(norm_gain, "exp", axis=0, tiled=True),
    )
    widened = full_rows.astype(jnp.float32)
    meansq = jnp.sum(widened * widened, axis=1, keepdims=True) / width_full
    normed = (widened * lax.rsqrt(meansq + 1e-06) * full_gain.astype(jnp.float32)[None, :]).astype(
        jnp.bfloat16
    )
    flat_ids = expert_ids.reshape(-1)
    matches = flat_ids[:, None] == flat_ids[None, :]
    earlier = lax.broadcasted_iota(jnp.int32, matches.shape, 1) < lax.broadcasted_iota(
        jnp.int32, matches.shape, 0
    )
    slot_index = jnp.sum((matches & earlier).astype(jnp.int32), axis=1).reshape(
        local_rows, top_count
    )
    target_codes = expert_ids * capacity + slot_index
    targets = lax.broadcasted_iota(jnp.int32, (experts_all * capacity, local_rows, top_count), 0)
    placed = (targets == target_codes[None, :, :]).astype(jnp.float32)
    dispatch = jnp.sum(placed, axis=2).astype(jnp.bfloat16)
    outgoing = jnp.dot(dispatch, normed, preferred_element_type=jnp.float32).astype(jnp.bfloat16)
    outgoing = outgoing.reshape(experts_all, capacity, normed.shape[1])
    arrived = lax.all_to_all(outgoing, "att", split_axis=0, concat_axis=0, tiled=True)
    arrived = arrived.reshape(owners, local_experts, capacity, width_full)
    gate_act = jnp.einsum("secd,edf->secf", arrived, gate_proj, preferred_element_type=jnp.float32)
    up_act = jnp.einsum("secd,edf->secf", arrived, up_proj, preferred_element_type=jnp.float32)
    inner_act = (jax.nn.silu(gate_act) * up_act).astype(jnp.bfloat16)
    partial_out = jnp.einsum(
        "secf,efd->secd", inner_act, down_proj, preferred_element_type=jnp.float32
    )
    returned = lax.psum_scatter(
        partial_out.astype(jnp.bfloat16), "exp", scatter_dimension=3, tiled=True
    )
    returned_rows = lax.all_to_all(returned, "att", split_axis=0, concat_axis=0, tiled=True)
    returned_rows = returned_rows.reshape(experts_all * capacity, returned_rows.shape[3]).astype(
        jnp.float32
    )
    share_norm = gate_probs / jnp.sum(gate_probs, axis=1, keepdims=True)
    combine_table = jnp.sum(placed * share_norm[None, :, :], axis=2)
    combined = jnp.dot(combine_table.T, returned_rows, precision=lax.Precision.HIGHEST)
    return (hidden.astype(jnp.float32) + combined).astype(jnp.bfloat16)


def solution(mesh):
    return jax.shard_map(
        body,
        mesh=mesh,
        in_specs=(
            P(("groups", "att"), "exp"),
            P(("groups", "att"), "exp", None, None),
            P(("groups", "att"), "exp", None, None),
            P(("groups", "att"), "exp"),
            P(("groups", "att"), "exp"),
            P(("groups", "att")),
            P(("groups", "att"), "exp"),
            P("exp"),
            P(("groups", "att"), None),
            P(("groups", "att"), None),
            P("att", None, "exp"),
            P("att", None, "exp"),
            P("att", "exp", None),
        ),
        out_specs=P(("groups", "att"), "exp"),
        check_vma=False,
    )
```

profile of v0, /device:TPU:0, one launch (start us, length us, event | category | flops | bytes accessed | tf_op | source)
XLA Modules:
  0.0 235.2 jit_solution(11122291866880856966)
XLA Ops:
  0.0 0.7 reduce_sum.56
  0.7 0.7 broadcast_divide_fusion
  1.4 0.1 copy.25
  1.5 0.8 copy.23
  2.2 0.1 eq.23
  2.3 0.2 convert_reduce_fusion.1
  2.5 0.1 reshape.68
  2.6 0.7 convert_element_type.77
  3.3 0.7 reshape.82
  4.1 0.7 reshape.75
  4.8 1.1 copy.29
  6.0 0.2 fusion.43
  6.2 3.5 %fusion.42 = (f32[32,2,16]{2,1,0:T(2,128)S(1)}, f32[32,2,16,256]{3,2,1,0:T(8,128)S(1)}) fusion(bf16[32,2,16,128]{3,2,1,0:T(8,128)(2,1)S(1)} %bitcast.94, bf16[32,2,256,128]{3,2,1,0:T(8,128)(2,1)} %param.14, s32[32]{0:T(128)} %param.18), kind=kOutput, calls=%fused_computation.54 | convolution fusion | flops 68156416 | bytes 5509248 | tf_op jit(solution)/shard_map/rghd,rgpd->rghp/dot_general | solution.py:17
  9.8 0.4 fusion.25
  10.3 0.8 convolution_add_fusion.1
  11.2 0.4 fusion.27
  11.6 0.4 convert_reduce_fusion
  12.0 1.3 convolution_convert_fusion
  13.3 99.6 %all_to_all.10 = bf16[16,32,4096]{2,1,0:T(8,128)(2,1)S(1)} all-to-all(bf16[16,32,4096]{2,1,0:T(8,128)(2,1)S(1)} %bitcast.92), channel_id=1, replica_groups=mesh['groups'=2,'att'=16,'exp'=1] {'att'}, dimensions={0} | all-to-all | bytes 8388608 | tf_op jit(solution)/shard_map/all_to_all | solution.py:88
  112.9 1.9 copy-done
  114.8 3.4 %fusion.4 = f32[16,32,768]{2,1,0:T(8,128)S(1)} fusion(bf16[16,32,4096]{2,1,0:T(8,128)(2,1)S(1)} %all_to_all.10, bf16[1,4096,768]{2,1,0:T(8,128)(2,1)S(1)} %bitcast.100), kind=kOutput, calls=%fused_computation.4 | convolution fusion | flops 3221225472 | bytes 12058624 | tf_op jit(solution)/shard_map/secd,edf->secf/dot_general | solution.py:90
  118.2 16.6 %fusion.9 = bf16[16,1,32,4096]{3,2,1,0:T(8,128)(2,1)} fusion(bf16[1,768,4096]{2,1,0:T(8,128)(2,1)} %param.25, bf16[16,32,4096]{2,1,0:T(8,128)(2,1)} %copy-done, bf16[1,4096,768]{2,1,0:T(8,128)(2,1)} %param.24, f32[16,32,768]{2,1,0:T(8,128)S(1)} %fusion.4), kind=kOutput, calls=%fused_computation.8 | convolution fusion | flops 6446907392 | bytes 22544384 | tf_op jit(solution)/shard_map/secf,efd->secd/dot_general | solution.py:93
  134.8 97.6 %all_to_all.11 = bf16[16,1,32,4096]{3,2,1,0:T(8,128)(2,1)S(1)} all-to-all(bf16[16,1,32,4096]{3,2,1,0:T(8,128)(2,1)} %fusion.9), channel_id=1, replica_groups=mesh['groups'=2,'att'=16,'exp'=1] {'att'}, dimensions={0} | all-to-all | bytes 8388608 | tf_op jit(solution)/shard_map/all_to_all | solution.py:99
  232.4 2.9 %fusion.12 = bf16[32,4096]{1,0:T(8,128)(2,1)} fusion(f32[512,32]{0,1:T(8,128)S(1)} %get-tuple-element.6, bf16[512,4096]{1,0:T(8,128)(2,1)S(1)} %bitcast.91, bf16[32,4096]{1,0:T(8,128)(2,1)S(1)} %get-tuple-element.8), kind=kOutput, calls=%fused_computation.10 | convolution fusion | flops 805699584 | bytes 4784128 | tf_op jit(solution)/shard_map/dot_general | solution.py:105
  (14 shorter events, 0.2 us)
Async XLA Ops:
  4.8 5.5 %copy-start.2 = (bf16[32,2,256,128]{3,2,1,0:T(8,128)(2,1)S(1)}, bf16[32,2,256,128]{3,2,1,0:T(8,128)(2,1)}, u32[]{:S(2)}) copy-start(bf16[32,2,256,128]{3,2,1,0:T(8,128)(2,1)} %param.15) | copy-start | bytes 12582916
  10.2 1.0 copy-start.1
  12.0 102.8 %slice-start = ((s8[6291456]{0:T(1024)(128)(4,1)}), s8[4194304]{0:T(1024)(128)(4,1)S(1)}, s32[]{:S(2)}) async-start(s8[6291456]{0:T(1024)(128)(4,1)} %bitcast.99), calls=%async_computation.2 | async-start | bytes 8388608
  13.3 101.5 %slice-start.1 = ((s8[6291456]{0:T(1024)(128)(4,1)}), s8[2097152]{0:T(1024)(128)(4,1)S(1)}, s32[]{:S(2)}) async-start(s8[6291456]{0:T(1024)(128)(4,1)} %bitcast.99), calls=%async_computation.3 | async-start | bytes 4194304
  112.9 1.9 copy-start
where the time goes:
time: 236 us; the launch traced here: 235 us
  blocking collectives  197 us (83%)
  matrix products  28.7 us (12%)
  local copies, waits for them, and re-layouts  5.62 us (2%)
  other arithmetic  3.64 us (2%)
    all_to_all x1, blocking collectives, body(): lax.all_to_all(outgoing, 'att', split_axis=0, concat_axis=0, tiled=True)  99.6 us
    all_to_all x1, blocking collectives, body(): lax.all_to_all(returned, 'att', split_axis=0, concat_axis=0, tiled=True)  97.6 us
    dot_general x1, matrix products, body(): jnp.einsum('secf,efd->secd', inner_act, down_proj, preferred_element_type...  16.6 us

commit v1 on v0

--- a/solution.py
+++ b/solution.py
@@ -106,9 +106,65 @@
     return (hidden.astype(jnp.float32) + combined).astype(jnp.bfloat16)
 
 
+def norm_rows(hidden, norm_gain):
+    widened = hidden.astype(jnp.float32)
+    meansq = jnp.sum(widened * widened, axis=1, keepdims=True) / hidden.shape[1]
+    return (widened * lax.rsqrt(meansq + 1e-06) * norm_gain.astype(jnp.float32)[None, :]).astype(
+        jnp.bfloat16
+    )
+
+
+def share_table(expert_ids, gate_probs, experts_all):
+    share_norm = gate_probs / jnp.sum(gate_probs, axis=1, keepdims=True)
+    hits = expert_ids[:, :, None] == jnp.arange(experts_all, dtype=jnp.int32)[None, None, :]
+    return jnp.sum(jnp.where(hits, share_norm[:, :, None], 0.0), axis=1)
+
+
+def dense_body(
+    queries,
+    key_cache,
+    value_cache,
+    new_key,
+    new_value,
+    lengths,
+    residual,
+    norm_gain,
+    expert_ids,
+    gate_probs,
+    gate_proj,
+    up_proj,
+    down_proj,
+):
+    attended = attend(queries, key_cache, value_cache, new_key, new_value, lengths)
+    hidden = (residual.astype(jnp.float32) + attended).astype(jnp.bfloat16)
+    normed = norm_rows(hidden, norm_gain)
+    owners = lax.axis_size("att")
+    me = lax.axis_index("att")
+    shares = share_table(expert_ids, gate_probs, owners)
+    all_shares = lax.all_gather(shares, "att", axis=0, tiled=True)
+    own_share = lax.dynamic_slice_in_dim(all_shares, me, 1, axis=1)
+    rows = lax.all_gather(normed, "att", axis=0, tiled=True)
+    gate_act = jnp.dot(rows, gate_proj[0], preferred_element_type=jnp.float32)
+    up_act = jnp.dot(rows, up_proj[0], preferred_element_type=jnp.float32)
+    inner_act = (jax.nn.silu(gate_act) * up_act).astype(jnp.bfloat16)
+    out = jnp.dot(inner_act, down_proj[0], preferred_element_type=jnp.float32)
+    weighted = (out.astype(jnp.bfloat16).astype(jnp.float32) * own_share).astype(jnp.bfloat16)
+    combined = lax.psum_scatter(weighted, "att", scatter_dimension=0, tiled=True)
+    return (hidden.astype(jnp.float32) + combined.astype(jnp.float32)).astype(jnp.bfloat16)
+
+
+def pick_body(*args):
+    local_rows, top_count = args[8].shape
+    experts_all = lax.axis_size("att") * args[10].shape[0]
+    capacity = min(local_rows, max(2, 2 * local_rows * top_count // experts_all))
+    if lax.axis_size("exp") == 1 and args[10].shape[0] == 1 and capacity == local_rows:
+        return dense_body(*args)
+    return body(*args)
+
+
 def solution(mesh):
     return jax.shard_map(
-        body,
+        pick_body,
         mesh=mesh,
         in_specs=(
             P(("groups", "att"), "exp"),

time: 236 us -> 174 us (0.74)
  blocking collectives: 197 us -> 23.8 us
  waiting for transfers between devices: 0 us -> 101 us
  between operations: 0.12 us -> 13.5 us
  local copies, waits for them, and re-layouts: 5.62 us -> 2.81 us
    all_to_all x2 -> x0, blocking collectives: 197 us -> none  [the longest x1 99.6 us: body(): lax.all_to_all(outgoing, 'att', split_axis=0, concat_axis=0, tiled=True)]
    reduce_scatter x0 -> x1, waiting for transfers between devices: none -> 71.2 us  [dense_body(): lax.psum_scatter(weighted, 'att', scatter_dimension=0, tiled=True)]
    all_gather x0 -> x1, waiting for transfers between devices: none -> 29.6 us  [dense_body(): rows = lax.all_gather(normed, 'att', axis=0, tiled=True)]
    all_gather x0 -> x1, blocking collectives: none -> 23.8 us  [dense_body(): all_shares = lax.all_gather(shares, 'att', axis=0, tiled=True)]
    unnamed x12 -> x10, local copies, waits for them, and re-layouts: 3.91 us -> 1.3 us
    convert_element_type x1 -> x3, other arithmetic: 0.7 us -> 3.25 us  [the longest x1 1.71 us: dense_body(): (hidden.astype(jnp.float32) + combined.astype(jnp.float32)).astype(jnp.bf...]
    dot_general x4 -> x2, matrix products: 24.2 us -> 23.6 us  [the longest x1 16.6 us: dense_body(): out = jnp.dot(inner_act, down_proj[0], preferred_element_type=jnp.float32)]
  transfers between devices with their start and end apart: 0 -> 2, of which waited for: 0 -> 2; matrix products, arithmetic and copies ran while one was open for 0% -> 0% of each run, Pallas kernels for 0% -> 0%
where the time goes in v1:
time: 174 us; the launch traced here: 173 us
  waiting for transfers between devices  101 us (58%)
  matrix products  28.2 us (16%)
  blocking collectives  23.8 us (14%)
  between operations  13.5 us (8%)
  other arithmetic  4.25 us (2%)
  local copies, waits for them, and re-layouts  2.81 us (2%)
    reduce_scatter x1, waiting for transfers between devices, dense_body(): lax.psum_scatter(weighted, 'att', scatter_dimension=0, tiled=True)  71.2 us
    all_gather x1, waiting for transfers between devices, dense_body(): rows = lax.all_gather(normed, 'att', axis=0, tiled=True)  29.6 us
    all_gather x1, blocking collectives, dense_body(): all_shares = lax.all_gather(shares, 'att', axis=0, tiled=True)  23.8 us
    dot_general x1, matrix products, dense_body(): out = jnp.dot(inner_act, down_proj[0], preferred_element_type=jnp.float32)  16.6 us
    dot_general x1, matrix products, dense_body(): gate_act = jnp.dot(rows, gate_proj[0], preferred_element_type=jnp.float32)  7.04 us
    dot_general x1, matrix products, attend(): jnp.einsum('rghd,rgpd->rghp', query_blocks, key_cache, preferred_element_...  3.51 us
  transfers between devices with their start and end apart: 2, of which 2 were waited for; matrix products, arithmetic and copies ran while one was open for 0% of the time, Pallas kernels for 0%

profile of v1, /device:TPU:0, one launch (start us, length us, event | category | flops | bytes accessed | tf_op | source)
XLA Modules:
  0.0 173.4 jit_solution(13850784230727130673)
XLA Ops:
  6.5 0.7 convert_element_type.61
  7.2 0.7 reshape.42
  8.0 0.7 reshape.36
  8.7 0.0 copy-start.3
  8.7 1.1 copy.26
  9.9 0.2 fusion.29
  10.1 3.5 %fusion.28 = (f32[32,2,16]{2,1,0:T(2,128)S(1)}, f32[32,2,16,256]{3,2,1,0:T(8,128)S(1)}) fusion(bf16[32,2,16,128]{3,2,1,0:T(8,128)(2,1)S(1)} %bitcast.41, bf16[32,2,256,128]{3,2,1,0:T(8,128)(2,1)} %param.14, s32[32]{0:T(128)} %param.18), kind=kOutput, calls=%fused_computation.38 | convolution fusion | flops 68156416 | bytes 5509248 | tf_op jit(solution)/shard_map/rghd,rgpd->rghp/dot_general | solution.py:17
  13.7 0.4 fusion.14
  14.1 0.1 fusion.24
  14.2 0.0 copy-start.1
  14.2 0.8 convolution_add_fusion
  15.0 0.0 copy-done
  15.1 0.4 fusion.17
  15.5 0.8 fusion.19
  16.3 0.0 all-gather.3.cloned.1.call-update
  16.4 0.0 reduce-scatter.2.cloned.1.call-start
  16.5 23.8 %all-gather = f32[16,32,16]{1,2,0:T(8,128)S(1)} all-gather(f32[1,32,16]{1,2,0:T(8,128)S(1)} %bitcast.46), channel_id=1, replica_groups=mesh['groups'=2,'att'=16,'exp'=1] {'att'}, dimensions={0}, use_global_device_ids=true | all-gather | bytes 34816 | tf_op jit(solution)/shard_map/all_gather | solution.py:144
  40.3 0.1 reshape.38
  40.4 29.6 %all-gather.3.cloned.1.call-done = bf16[512,4096]{1,0:T(8,128)(2,1)} async-done(((bf16[32,4096]{1,0:T(8,128)(2,1)}), bf16[512,4096]{1,0:T(8,128)(2,1)}) %all-gather.3.cloned.1.call-update) | async-done | bytes 4194320 | tf_op jit(solution)/shard_map/all_gather | solution.py:146
  70.0 7.0 %fusion.4 = f32[512,768]{1,0:T(8,128)S(1)} fusion(bf16[512,4096]{1,0:T(8,128)(2,1)} %all-gather.3.cloned.1.call-done, bf16[1,4096,768]{2,1,0:T(8,128)(2,1)} %param.23), kind=kOutput, calls=%fused_computation.5 | convolution fusion | flops 3221225472 | bytes 12058624 | tf_op jit(solution)/shard_map/dot_general | solution.py:147
  77.1 16.6 %multiply_convert_fusion = bf16[512,4096]{1,0:T(8,128)(2,1)} fusion(bf16[1,768,4096]{2,1,0:T(8,128)(2,1)} %param.25, f32[512]{0:T(512)S(1)} %bitcast.47, f32[512,768]{1,0:T(8,128)S(1)} %fusion.4, bf16[512,4096]{1,0:T(8,128)(2,1)} %all-gather.3.cloned.1.call-done, bf16[1,4096,768]{2,1,0:T(8,128)(2,1)} %param.24), kind=kOutput, calls=%fused_computation | convolution fusion | flops 6453198848 | bytes 22546432 | tf_op jit(solution)/shard_map/dot_general | solution.py:150
  93.7 0.0 reduce-scatter.2.cloned.1.call-update
  93.7 71.2 %reduce-scatter.2.cloned.1.call-done = bf16[32,4096]{1,0:T(8,128)(2,1)} async-done(((bf16[512,4096]{1,0:T(8,128)(2,1)}), bf16[32,4096]{1,0:T(8,128)(2,1)}) %reduce-scatter.2.cloned.1.call-update) | async-done | bytes 262160 | tf_op jit(solution)/shard_map/reduce_scatter | solution.py:152
  164.9 1.7 fusion.20
  (13 shorter events, 0.1 us)
Async XLA Ops:
  6.5 63.5 %all-gather.3.cloned.1.call-start = ((), (), s32[]{:S(2)}) async-start(), calls=%async_computation.1 | async-start | bytes 4456448 | tf_op jit(solution)/shard_map/all_gather | solution.py:146
  8.7 5.5 %copy-start.3 = (bf16[32,2,256,128]{3,2,1,0:T(8,128)(2,1)S(1)}, bf16[32,2,256,128]{3,2,1,0:T(8,128)(2,1)}, u32[]{:S(2)}) copy-start(bf16[32,2,256,128]{3,2,1,0:T(8,128)(2,1)} %param.15) | copy-start | bytes 12582916
  14.1 1.0 copy-start
  14.2 2.2 %copy-start.1 = (f32[32,8]{0,1:T(8,128)S(1)}, f32[32,8]{0,1:T(8,128)}, u32[]{:S(2)}) copy-start(f32[32,8]{0,1:T(8,128)} %param.22) | copy-start | bytes 3076
  14.2 2.2 %copy-start.2 = (s32[32,8]{0,1:T(8,128)S(1)}, s32[32,8]{0,1:T(8,128)}, u32[]{:S(2)}) copy-start(s32[32,8]{0,1:T(8,128)} %param.21) | copy-start | bytes 3076
  16.4 148.5 %reduce-scatter.2.cloned.1.call-start = ((), (), s32[]{:S(2)}) async-start(), calls=%async_computation.2 | async-start | bytes 4456448 | tf_op jit(solution)/shard_map/reduce_scatter | solution.py:152
Sparse Core Ops, SparseCore 0:
  16.5 53.5 all-gather.2
  93.8 71.0 reduce-scatter.1

commit v2 on v1

--- a/solution.py
+++ b/solution.py
@@ -3,6 +3,8 @@
 import jax
 import jax.numpy as jnp
 from jax import lax
+from jax.experimental import pallas as pl
+from jax.experimental.pallas import tpu as pltpu
 from jax.sharding import PartitionSpec as P
 
 
@@ -120,6 +122,160 @@
     return jnp.sum(jnp.where(hits, share_norm[:, :, None], 0.0), axis=1)
 
 
+def expert_kernel(
+    block_ref,
+    hidden_ref,
+    gate_hbm,
+    up_hbm,
+    down_hbm,
+    out_ref,
+    rows,
+    part,
+    got,
+    inner,
+    gate,
+    up,
+    down,
+    weight_sem,
+    row_send,
+    row_recv,
+    sum_send,
+    sum_recv,
+):
+    me = lax.axis_index("att")
+    partners = {m: me + m - 2 * m * (lax.div(me, m) % 2) for m in (1, 2, 4, 8)}
+    block_rows, width = hidden_ref.shape
+
+    barrier = pltpu.get_barrier_semaphore()
+    for m in (1, 2, 4, 8):
+        pl.semaphore_signal(
+            barrier, inc=1, device_id={"att": partners[m]}, device_id_type=pl.DeviceIdType.MESH
+        )
+    loads = [
+        pltpu.make_async_copy(source, held, weight_sem.at[i])
+        for i, (source, held) in enumerate(((gate_hbm, gate), (up_hbm, up), (down_hbm, down)))
+    ]
+    for load in loads:
+        load.start()
+    pl.semaphore_wait(barrier, 4)
+
+    sent = {}
+
+    def forward(slot, *masks):
+        for m in masks:
+            copy = pltpu.make_async_remote_copy(
+                src_ref=block_ref if slot == 0 else rows.at[slot],
+                dst_ref=rows.at[slot + m],
+                send_sem=row_send.at[slot + m],
+                recv_sem=row_recv.at[slot + m],
+                device_id={"att": partners[m]},
+                device_id_type=pl.DeviceIdType.MESH,
+            )
+            copy.start()
+            sent["row", slot + m] = copy
+
+    def arrived(*slots):
+        for slot in slots:
+            sent["row", slot].wait_recv()
+
+    def send_sum(slot, m, place):
+        copy = pltpu.make_async_remote_copy(
+            src_ref=part.at[slot],
+            dst_ref=got.at[place],
+            send_sem=sum_send.at[place],
+            recv_sem=sum_recv.at[place],
+            device_id={"att": partners[m]},
+            device_id_type=pl.DeviceIdType.MESH,
+        )
+        copy.start()
+        sent["sum", place] = copy
+
+    def add(slot, place):
+        sent["sum", place].wait_recv()
+        part[slot] = (part[slot].astype(jnp.float32) + got[place].astype(jnp.float32)).astype(
+            jnp.bfloat16
+        )
+
+    def experts(chunk):
+        first, count = 4 * chunk, 4
+        length = count * block_rows
+
+        def hidden_step(j, carry):
+            columns = pl.ds(pl.multiple_of(j * 256, 256), 256)
+            held = rows[first : first + count, :, :width].reshape(length, width)
+            g = jnp.dot(held, gate[:, columns], preferred_element_type=jnp.float32)
+            u = jnp.dot(held, up[:, columns], preferred_element_type=jnp.float32)
+            inner[:, columns] = (g / (1.0 + jnp.exp(-g)) * u).astype(jnp.bfloat16)
+            return carry
+
+        lax.fori_loop(0, gate.shape[1] // 256, hidden_step, 0)
+        pieces = rows[first : first + count, :, width:].reshape(length, 128).astype(jnp.float32)
+        lane = lax.broadcasted_iota(jnp.int32, pieces.shape, 1)
+        mine = (lane == me) | (lane == me + 16) | (lane == me + 32)
+        share = jnp.sum(jnp.where(mine, pieces, 0.0), axis=1, keepdims=True)
+
+        def out_step(j, carry):
+            columns = pl.ds(pl.multiple_of(j * 512, 512), 512)
+            o = jnp.dot(inner[...], down[:, columns], preferred_element_type=jnp.float32)
+            o = (o.astype(jnp.bfloat16).astype(jnp.float32) * share).astype(jnp.bfloat16)
+            part[first : first + count, :, columns] = o.reshape(count, block_rows, 512)
+            return carry
+
+        lax.fori_loop(0, width // 512, out_step, 0)
+        for xr in (0, 1):
+            send_sum(first + 2 * xr + 1, 1, 2 * chunk + xr)
+
+    def across_x(chunk):
+        add(4 * chunk + 2, 2 * chunk + 1)
+        send_sum(4 * chunk + 2, 2, 8 + chunk)
+        add(4 * chunk, 2 * chunk)
+
+    forward(0, 2, 4, 8, 1)
+    rows[0] = block_ref[...]
+    arrived(4)
+    forward(4, 2, 8, 1)
+    arrived(2)
+    forward(2, 1)
+    arrived(8)
+    forward(8, 2, 1)
+    for load in loads:
+        load.wait()
+    arrived(1, 3)
+    experts(0)
+    arrived(6)
+    forward(6, 1)
+    arrived(12)
+    forward(12, 2, 1)
+    across_x(0)
+    arrived(5, 7)
+    experts(1)
+    arrived(10)
+    forward(10, 1)
+    across_x(1)
+    arrived(9, 11)
+    experts(2)
+    arrived(14)
+    forward(14, 1)
+    across_x(2)
+    arrived(13, 15)
+    experts(3)
+    across_x(3)
+    add(8, 10)
+    send_sum(8, 8, 12)
+    add(12, 11)
+    send_sum(12, 8, 13)
+    add(0, 8)
+    add(4, 9)
+    add(4, 13)
+    send_sum(4, 4, 14)
+    add(0, 12)
+    sent["sum", 14].wait_recv()
+    total = part[0].astype(jnp.float32) + got[14].astype(jnp.float32)
+    out_ref[...] = (hidden_ref[...].astype(jnp.float32) + total).astype(jnp.bfloat16)
+    for copy in sent.values():
+        copy.wait_send()
+
+
 def dense_body(
     queries,
     key_cache,
@@ -139,25 +295,54 @@
     hidden = (residual.astype(jnp.float32) + attended).astype(jnp.bfloat16)
     normed = norm_rows(hidden, norm_gain)
     owners = lax.axis_size("att")
-    me = lax.axis_index("att")
-    shares = share_table(expert_ids, gate_probs, owners)
-    all_shares = lax.all_gather(shares, "att", axis=0, tiled=True)
-    own_share = lax.dynamic_slice_in_dim(all_shares, me, 1, axis=1)
-    rows = lax.all_gather(normed, "att", axis=0, tiled=True)
-    gate_act = jnp.dot(rows, gate_proj[0], preferred_element_type=jnp.float32)
-    up_act = jnp.dot(rows, up_proj[0], preferred_element_type=jnp.float32)
-    inner_act = (jax.nn.silu(gate_act) * up_act).astype(jnp.bfloat16)
-    out = jnp.dot(inner_act, down_proj[0], preferred_element_type=jnp.float32)
-    weighted = (out.astype(jnp.bfloat16).astype(jnp.float32) * own_share).astype(jnp.bfloat16)
-    combined = lax.psum_scatter(weighted, "att", scatter_dimension=0, tiled=True)
-    return (hidden.astype(jnp.float32) + combined.astype(jnp.float32)).astype(jnp.bfloat16)
+    local_rows, width = hidden.shape
+    units = gate_proj.shape[2]
+    rest, terms = share_table(expert_ids, gate_probs, owners), []
+    for _ in range(3):
+        term = lax.reduce_precision(rest, 8, 7)
+        terms.append(term.astype(jnp.bfloat16))
+        rest = rest - term
+    spare = jnp.zeros((local_rows, 128 - 3 * owners), jnp.bfloat16)
+    block = jnp.concatenate([normed, *terms, spare], axis=1)
+    weight = gate_proj.size + up_proj.size + down_proj.size
+    vmem = pl.BlockSpec(memory_space=pltpu.VMEM)
+    hbm = pl.BlockSpec(memory_space=pl.ANY)
+    return pl.pallas_call(
+        expert_kernel,
+        out_shape=jax.ShapeDtypeStruct((local_rows, width), jnp.bfloat16),
+        in_specs=[vmem, vmem, hbm, hbm, hbm],
+        out_specs=vmem,
+        scratch_shapes=[
+            pltpu.VMEM((owners, local_rows, block.shape[1]), jnp.bfloat16),
+            pltpu.VMEM((owners, local_rows, width), jnp.bfloat16),
+            pltpu.VMEM((owners, local_rows, width), jnp.bfloat16),
+            pltpu.VMEM((4 * local_rows, units), jnp.bfloat16),
+            pltpu.VMEM((width, units), jnp.bfloat16),
+            pltpu.VMEM((width, units), jnp.bfloat16),
+            pltpu.VMEM((units, width), jnp.bfloat16),
+            pltpu.SemaphoreType.DMA((3,)),
+            pltpu.SemaphoreType.DMA((16,)),
+            pltpu.SemaphoreType.DMA((16,)),
+            pltpu.SemaphoreType.DMA((16,)),
+            pltpu.SemaphoreType.DMA((16,)),
+        ],
+        compiler_params=pltpu.CompilerParams(
+            collective_id=0, has_side_effects=True, vmem_limit_bytes=48 * 1024 * 1024
+        ),
+        cost_estimate=pl.CostEstimate(
+            flops=2 * owners * local_rows * weight,
+            bytes_accessed=2 * weight,
+            transcendentals=owners * local_rows * units,
+        ),
+    )(block, hidden, gate_proj[0], up_proj[0], down_proj[0])
 
 
 def pick_body(*args):
     local_rows, top_count = args[8].shape
     experts_all = lax.axis_size("att") * args[10].shape[0]
     capacity = min(local_rows, max(2, 2 * local_rows * top_count // experts_all))
-    if lax.axis_size("exp") == 1 and args[10].shape[0] == 1 and capacity == local_rows:
+    dense = lax.axis_size("exp") == 1 and args[10].shape[0] == 1 and capacity == local_rows
+    if dense and lax.axis_size("att") == 16:
         return dense_body(*args)
     return body(*args)
 

time: 174 us -> 90.8 us (0.52)
  waiting for transfers between devices: 101 us -> 0 us
  Pallas kernels: 0 us -> 80.6 us
  blocking collectives: 23.8 us -> 0 us
  matrix products: 28.2 us -> 6.7 us
  between operations: 13.5 us -> 0.17 us
  other arithmetic: 4.25 us -> 1.15 us
    pallas_call x0 -> x1, Pallas kernels: none -> 80.6 us  [dense_body(): pl.pallas_call(expert_kernel, out_shape=jax.ShapeDtypeStruct((local_rows,...]
    reduce_scatter x1 -> x0, waiting for transfers between devices: 71.2 us -> none  [dense_body(): lax.psum_scatter(weighted, 'att', scatter_dimension=0, tiled=True)]
    all_gather x1 -> x0, waiting for transfers between devices: 29.6 us -> none  [dense_body(): rows = lax.all_gather(normed, 'att', axis=0, tiled=True)]
    all_gather x1 -> x0, blocking collectives: 23.8 us -> none  [dense_body(): all_shares = lax.all_gather(shares, 'att', axis=0, tiled=True)]
    dot_general x2 -> x0, matrix products: 23.6 us -> none  [the longest x1 16.6 us: dense_body(): out = jnp.dot(inner_act, down_proj[0], preferred_element_type=jnp.float32)]
    dot_general x1, matrix products: 0.82 us -> 2.96 us  [attend(): jnp.einsum('rghp,rgpd->rghd', weights, value_cache, preferred_element_typ...]
  transfers between devices with their start and end apart: 2 -> 0, of which waited for: 2 -> 0; matrix products, arithmetic and copies ran while one was open for 0% -> 0% of each run, Pallas kernels for 0% -> 0%
where the time goes in v2:
time: 90.8 us; the launch traced here: 90.7 us
  Pallas kernels  80.6 us (89%)
  matrix products  6.7 us (7%)
  local copies, waits for them, and re-layouts  2.03 us (2%)
  other arithmetic  1.15 us (1%)
    pallas_call x1, Pallas kernels, dense_body(): pl.pallas_call(expert_kernel, out_shape=jax.ShapeDtypeStruct((local_rows,...  80.6 us
    dot_general x1, matrix products, attend(): jnp.einsum('rghd,rgpd->rghp', query_blocks, key_cache, preferred_element_...  3.49 us
    dot_general x1, matrix products, attend(): jnp.einsum('rghp,rgpd->rghd', weights, value_cache, preferred_element_typ...  2.96 us

profile of v2, /device:TPU:0, one launch (start us, length us, event | category | flops | bytes accessed | tf_op | source)
XLA Modules:
  0.0 90.7 jit_solution(11457695568175978769)
XLA Ops:
  0.0 0.0 copy-start.1
  0.0 1.0 %copy.23 = bf16[4,8,32,128]{3,2,1,0:T(8,128)(2,1)S(1)} copy(bf16[4,8,32,128]{3,1,2,0:T(8,128)(2,1)} %bitcast.23) | data formatting | bytes 524288
  1.0 3.5 %fusion.13 = (f32[32,2,16]{2,1,0:T(2,128)S(1)}, f32[32,2,16,256]{3,2,1,0:T(8,128)S(1)}) fusion(bf16[32,2,16,128]{3,2,1,0:T(8,128)(2,1)S(1)} %bitcast.20, bf16[32,2,256,128]{3,2,1,0:T(8,128)(2,1)} %param.14, s32[32]{0:T(128)} %param.18), kind=kOutput, calls=%fused_computation.29 | convolution fusion | flops 68156416 | bytes 5509248 | tf_op jit(solution)/shard_map/rghd,rgpd->rghp/dot_general | solution.py:19
  4.5 0.0 copy-done.1
  4.5 0.2 fusion.14
  4.8 0.4 fusion.1
  5.3 0.0 copy-start
  5.3 0.1 fusion.10
  5.3 0.0 copy-done.2
  5.4 0.0 copy-start.4
  5.4 0.0 copy-start.3
  5.4 0.0 copy-start.5
  5.4 3.0 %convolution_add_fusion = f32[32,2,16,128]{3,2,1,0:T(8,128)S(1)} fusion(bf16[32,2,256,128]{3,2,1,0:T(8,128)(2,1)} %param.15, f32[32,2,16,256]{3,2,1,0:T(8,128)S(1)} %get-tuple-element.13, f32[32,2,16]{2,1,0:T(2,128)S(1)} %get-tuple-element.8, f32[32,2,16]{2,1,0:T(2,128)S(1)} %multiply_maximum_fusion, f32[32,2,128]{2,1,0:T(2,128)S(1)} %reshape.36, ...), kind=kOutput, calls=%fused_computation.2 | convolution fusion | flops 68157440 | bytes 5812224 | tf_op jit(solution)/shard_map/rghp,rgpd->rghd/dot_general | solution.py:37
  8.4 0.0 copy-done
  8.4 0.4 fusion.2
  8.8 0.0 copy-done.4
  8.8 0.1 fusion.4
  9.0 0.0 copy-done.3
  9.0 0.0 copy-done.5
  9.1 0.1 copy.18
  9.1 0.1 copy.19
  9.2 0.1 concatenate.3.block_ref
  9.3 80.6 %shard_map.127 = bf16[32,4096]{1,0:T(8,128)(2,1)S(1)} custom-call(bf16[32,4224]{1,0:T(8,128)(2,1)S(1)} %concatenate.3.block_ref, bf16[32,4096]{1,0:T(8,128)(2,1)S(1)} %get-tuple-element.6.hidden_ref, bf16[4096,768]{1,0:T(8,128)(2,1)} %bitcast.26, bf16[4096,768]{1,0:T(8,128)(2,1)} %bitcast.27, bf16[768,4096]{1,0:T(8,128)(2,1)} %bitcast.28), custom_call_target="tpu_custom_call" | custom-call | flops 9663676416 | bytes 18874368 | tf_op jit(solution)/shard_map/pallas_call | solution.py:310
  90.0 0.7 copy.28
  (12 shorter events, 0.1 us)
Async XLA Ops:
  0.0 4.5 %copy-start.1 = (bf16[32,256]{1,0:T(8,128)(2,1)S(1)}, bf16[32,256]{1,0:T(8,128)(2,1)}, u32[]{:S(2)}) copy-start(bf16[32,256]{1,0:T(8,128)(2,1)} %param.16) | copy-start | bytes 49156
  0.0 5.3 %copy-start.2 = (bf16[32,256]{1,0:T(8,128)(2,1)S(1)}, bf16[32,256]{1,0:T(8,128)(2,1)}, u32[]{:S(2)}) copy-start(bf16[32,256]{1,0:T(8,128)(2,1)} %param.17) | copy-start | bytes 49156
  5.3 3.1 %copy-start = (bf16[32,4096]{1,0:T(8,128)(2,1)S(1)}, bf16[32,4096]{1,0:T(8,128)(2,1)}, u32[]{:S(2)}) copy-start(bf16[32,4096]{1,0:T(8,128)(2,1)} %param.19) | copy-start | bytes 786436
  5.4 3.4 %copy-start.4 = (bf16[4096]{0:T(1024)(128)(2,1)S(1)}, bf16[4096]{0:T(1024)(128)(2,1)}, u32[]{:S(2)}) copy-start(bf16[4096]{0:T(1024)(128)(2,1)} %param.20) | copy-start | bytes 24580
  5.4 3.6 %copy-start.3 = (f32[32,8]{0,1:T(8,128)S(1)}, f32[32,8]{0,1:T(8,128)}, u32[]{:S(2)}) copy-start(f32[32,8]{0,1:T(8,128)} %param.22) | copy-start | bytes 3076
  5.4 3.6 %copy-start.5 = (s32[32,8]{0,1:T(8,128)S(1)}, s32[32,8]{0,1:T(8,128)}, u32[]{:S(2)}) copy-start(s32[32,8]{0,1:T(8,128)} %param.21) | copy-start | bytes 3076

commit v3 on v2

--- a/solution.py
+++ b/solution.py
@@ -1,3 +1,4 @@
+import functools
 import math
 
 import jax
@@ -137,17 +138,19 @@
     up,
     down,
     weight_sem,
-    row_send,
+    send_sem,
     row_recv,
-    sum_send,
     sum_recv,
 ):
     me = lax.axis_index("att")
-    partners = {m: me + m - 2 * m * (lax.div(me, m) % 2) for m in (1, 2, 4, 8)}
+    layer = lax.div(me, 4)
+    inner_z = (layer == 1) | (layer == 2)
+    partners = {m: me + m - 2 * m * (lax.div(me, m) % 2) for m in (1, 2, 4)}
+    partners[12] = me + 4 * (3 - 2 * layer)
     block_rows, width = hidden_ref.shape
 
     barrier = pltpu.get_barrier_semaphore()
-    for m in (1, 2, 4, 8):
+    for m in (1, 2, 4, 12):
         pl.semaphore_signal(
             barrier, inc=1, device_id={"att": partners[m]}, device_id_type=pl.DeviceIdType.MESH
         )
@@ -159,39 +162,61 @@
         load.start()
     pl.semaphore_wait(barrier, 4)
 
-    sent = {}
-
-    def forward(slot, *masks):
+    sent = []
+
+    def start(copy, when):
+        sent.append((copy, when))
+        if when is None:
+            copy.start()
+        else:
+            pl.when(when)(copy.start)
+
+    def forward(slot, *masks, when=None):
         for m in masks:
             copy = pltpu.make_async_remote_copy(
                 src_ref=block_ref if slot == 0 else rows.at[slot],
-                dst_ref=rows.at[slot + m],
-                send_sem=row_send.at[slot + m],
-                recv_sem=row_recv.at[slot + m],
+                dst_ref=rows.at[slot ^ m],
+                send_sem=send_sem.at[len(sent)],
+                recv_sem=row_recv.at[slot ^ m],
                 device_id={"att": partners[m]},
                 device_id_type=pl.DeviceIdType.MESH,
             )
-            copy.start()
-            sent["row", slot + m] = copy
+            start(copy, when)
 
     def arrived(*slots):
         for slot in slots:
-            sent["row", slot].wait_recv()
-
-    def send_sum(slot, m, place):
+            pltpu.make_async_remote_copy(
+                src_ref=rows.at[slot],
+                dst_ref=rows.at[slot],
+                send_sem=row_recv.at[slot],
+                recv_sem=row_recv.at[slot],
+                device_id={"att": partners[1]},
+                device_id_type=pl.DeviceIdType.MESH,
+            ).wait_recv()
+
+    def send_sum(slot, m, place, when=None):
         copy = pltpu.make_async_remote_copy(
             src_ref=part.at[slot],
             dst_ref=got.at[place],
-            send_sem=sum_send.at[place],
+            send_sem=send_sem.at[len(sent)],
             recv_sem=sum_recv.at[place],
             device_id={"att": partners[m]},
             device_id_type=pl.DeviceIdType.MESH,
         )
-        copy.start()
-        sent["sum", place] = copy
+        start(copy, when)
+
+    def sum_arrived(place):
+        pltpu.make_async_remote_copy(
+            src_ref=got.at[place],
+            dst_ref=got.at[place],
+            send_sem=sum_recv.at[place],
+            recv_sem=sum_recv.at[place],
+            device_id={"att": partners[1]},
+            device_id_type=pl.DeviceIdType.MESH,
+        ).wait_recv()
 
     def add(slot, place):
-        sent["sum", place].wait_recv()
+        sum_arrived(place)
         part[slot] = (part[slot].astype(jnp.float32) + got[place].astype(jnp.float32)).astype(
             jnp.bfloat16
         )
@@ -230,50 +255,66 @@
         send_sum(4 * chunk + 2, 2, 8 + chunk)
         add(4 * chunk, 2 * chunk)
 
-    forward(0, 2, 4, 8, 1)
+    outer_z = jnp.logical_not(inner_z)
+    forward(0, 2, 4)
+    forward(0, 12, when=inner_z)
+    forward(0, 1)
     rows[0] = block_ref[...]
     arrived(4)
-    forward(4, 2, 8, 1)
+    forward(4, 2)
+    forward(4, 12, when=inner_z)
+    forward(4, 1)
+    pl.when(inner_z)(functools.partial(arrived, 12))
+    forward(12, 4, when=inner_z)
     arrived(2)
     forward(2, 1)
-    arrived(8)
-    forward(8, 2, 1)
     for load in loads:
         load.wait()
     arrived(1, 3)
     experts(0)
+    arrived(8)
+    forward(8, 2)
+    forward(8, 4, when=inner_z)
+    forward(8, 1)
     arrived(6)
     forward(6, 1)
-    arrived(12)
-    forward(12, 2, 1)
-    across_x(0)
     arrived(5, 7)
     experts(1)
+    pl.when(outer_z)(functools.partial(arrived, 12))
+    forward(12, 2, 1)
     arrived(10)
     forward(10, 1)
-    across_x(1)
     arrived(9, 11)
     experts(2)
+    across_x(2)
     arrived(14)
     forward(14, 1)
-    across_x(2)
     arrived(13, 15)
     experts(3)
     across_x(3)
+    across_x(1)
     add(8, 10)
-    send_sum(8, 8, 12)
+    send_sum(8, 4, 12, when=outer_z)
     add(12, 11)
-    send_sum(12, 8, 13)
+    send_sum(12, 4, 13, when=outer_z)
+    across_x(0)
+    pl.when(inner_z)(functools.partial(add, 12, 12))
+    send_sum(12, 12, 15, when=inner_z)
+    pl.when(inner_z)(functools.partial(add, 8, 13))
+    send_sum(8, 12, 16, when=inner_z)
+    add(4, 9)
+    pl.when(inner_z)(functools.partial(add, 4, 16))
+    send_sum(4, 4, 14)
     add(0, 8)
-    add(4, 9)
-    add(4, 13)
-    send_sum(4, 4, 14)
-    add(0, 12)
-    sent["sum", 14].wait_recv()
+    pl.when(inner_z)(functools.partial(add, 0, 15))
+    sum_arrived(14)
     total = part[0].astype(jnp.float32) + got[14].astype(jnp.float32)
     out_ref[...] = (hidden_ref[...].astype(jnp.float32) + total).astype(jnp.bfloat16)
-    for copy in sent.values():
-        copy.wait_send()
+    for copy, when in sent:
+        if when is None:
+            copy.wait_send()
+        else:
+            pl.when(when)(copy.wait_send)
 
 
 def dense_body(
@@ -315,16 +356,15 @@
         scratch_shapes=[
             pltpu.VMEM((owners, local_rows, block.shape[1]), jnp.bfloat16),
             pltpu.VMEM((owners, local_rows, width), jnp.bfloat16),
-            pltpu.VMEM((owners, local_rows, width), jnp.bfloat16),
+            pltpu.VMEM((17, local_rows, width), jnp.bfloat16),
             pltpu.VMEM((4 * local_rows, units), jnp.bfloat16),
             pltpu.VMEM((width, units), jnp.bfloat16),
             pltpu.VMEM((width, units), jnp.bfloat16),
             pltpu.VMEM((units, width), jnp.bfloat16),
             pltpu.SemaphoreType.DMA((3,)),
+            pltpu.SemaphoreType.DMA((40,)),
             pltpu.SemaphoreType.DMA((16,)),
-            pltpu.SemaphoreType.DMA((16,)),
-            pltpu.SemaphoreType.DMA((16,)),
-            pltpu.SemaphoreType.DMA((16,)),
+            pltpu.SemaphoreType.DMA((17,)),
         ],
         compiler_params=pltpu.CompilerParams(
             collective_id=0, has_side_effects=True, vmem_limit_bytes=48 * 1024 * 1024

time: 90.8 us -> 80.7 us (0.89)
  Pallas kernels: 80.6 us -> 70.5 us
    pallas_call x1, Pallas kernels: 80.6 us -> 70.5 us  [dense_body(): pl.pallas_call(expert_kernel, out_shape=jax.ShapeDtypeStruct((local_rows,...]
where the time goes in v3:
time: 80.7 us; the launch traced here: 80.5 us
  Pallas kernels  70.5 us (87%)
  matrix products  6.7 us (8%)
  local copies, waits for them, and re-layouts  2.03 us (3%)
  other arithmetic  1.15 us (1%)
    pallas_call x1, Pallas kernels, dense_body(): pl.pallas_call(expert_kernel, out_shape=jax.ShapeDtypeStruct((local_rows,...  70.5 us
    dot_general x1, matrix products, attend(): jnp.einsum('rghd,rgpd->rghp', query_blocks, key_cache, preferred_element_...  3.49 us
    dot_general x1, matrix products, attend(): jnp.einsum('rghp,rgpd->rghd', weights, value_cache, preferred_element_typ...  2.96 us
    unnamed x14, local copies, waits for them, and re-layouts  1.74 us

profile of v3, /device:TPU:0, one launch (start us, length us, event | category | flops | bytes accessed | tf_op | source)
XLA Modules:
  0.0 80.5 jit_solution(4292859745244456287)
XLA Ops:
  0.0 0.0 copy-start.1
  0.0 1.0 %copy.23 = bf16[4,8,32,128]{3,2,1,0:T(8,128)(2,1)S(1)} copy(bf16[4,8,32,128]{3,1,2,0:T(8,128)(2,1)} %bitcast.23) | data formatting | bytes 524288
  1.0 3.5 %fusion.13 = (f32[32,2,16]{2,1,0:T(2,128)S(1)}, f32[32,2,16,256]{3,2,1,0:T(8,128)S(1)}) fusion(bf16[32,2,16,128]{3,2,1,0:T(8,128)(2,1)S(1)} %bitcast.20, bf16[32,2,256,128]{3,2,1,0:T(8,128)(2,1)} %param.14, s32[32]{0:T(128)} %param.18), kind=kOutput, calls=%fused_computation.29 | convolution fusion | flops 68156416 | bytes 5509248 | tf_op jit(solution)/shard_map/rghd,rgpd->rghp/dot_general | solution.py:20
  4.5 0.0 copy-done.1
  4.5 0.2 fusion.14
  4.8 0.4 fusion.1
  5.3 0.0 copy-start
  5.3 0.1 fusion.10
  5.3 0.0 copy-done.2
  5.4 0.0 copy-start.4
  5.4 0.0 copy-start.3
  5.4 0.0 copy-start.5
  5.4 3.0 %convolution_add_fusion = f32[32,2,16,128]{3,2,1,0:T(8,128)S(1)} fusion(bf16[32,2,256,128]{3,2,1,0:T(8,128)(2,1)} %param.15, f32[32,2,16,256]{3,2,1,0:T(8,128)S(1)} %get-tuple-element.13, f32[32,2,16]{2,1,0:T(2,128)S(1)} %get-tuple-element.8, f32[32,2,16]{2,1,0:T(2,128)S(1)} %multiply_maximum_fusion, f32[32,2,128]{2,1,0:T(2,128)S(1)} %reshape.36, ...), kind=kOutput, calls=%fused_computation.2 | convolution fusion | flops 68157440 | bytes 5812224 | tf_op jit(solution)/shard_map/rghp,rgpd->rghd/dot_general | solution.py:38
  8.4 0.0 copy-done
  8.4 0.4 fusion.2
  8.8 0.0 copy-done.4
  8.8 0.1 fusion.4
  9.0 0.0 copy-done.3
  9.0 0.0 copy-done.5
  9.1 0.1 copy.18
  9.1 0.1 copy.19
  9.2 0.1 concatenate.3.block_ref
  9.3 70.5 %shard_map.127 = bf16[32,4096]{1,0:T(8,128)(2,1)S(1)} custom-call(bf16[32,4224]{1,0:T(8,128)(2,1)S(1)} %concatenate.3.block_ref, bf16[32,4096]{1,0:T(8,128)(2,1)S(1)} %get-tuple-element.6.hidden_ref, bf16[4096,768]{1,0:T(8,128)(2,1)} %bitcast.26, bf16[4096,768]{1,0:T(8,128)(2,1)} %bitcast.27, bf16[768,4096]{1,0:T(8,128)(2,1)} %bitcast.28), custom_call_target="tpu_custom_call" | custom-call | flops 9663676416 | bytes 18874368 | tf_op jit(solution)/shard_map/pallas_call | solution.py:351
  79.8 0.7 copy.28
  (12 shorter events, 0.1 us)
Async XLA Ops:
  0.0 4.5 %copy-start.1 = (bf16[32,256]{1,0:T(8,128)(2,1)S(1)}, bf16[32,256]{1,0:T(8,128)(2,1)}, u32[]{:S(2)}) copy-start(bf16[32,256]{1,0:T(8,128)(2,1)} %param.16) | copy-start | bytes 49156
  0.0 5.3 %copy-start.2 = (bf16[32,256]{1,0:T(8,128)(2,1)S(1)}, bf16[32,256]{1,0:T(8,128)(2,1)}, u32[]{:S(2)}) copy-start(bf16[32,256]{1,0:T(8,128)(2,1)} %param.17) | copy-start | bytes 49156
  5.3 3.1 %copy-start = (bf16[32,4096]{1,0:T(8,128)(2,1)S(1)}, bf16[32,4096]{1,0:T(8,128)(2,1)}, u32[]{:S(2)}) copy-start(bf16[32,4096]{1,0:T(8,128)(2,1)} %param.19) | copy-start | bytes 786436
  5.4 3.4 %copy-start.4 = (bf16[4096]{0:T(1024)(128)(2,1)S(1)}, bf16[4096]{0:T(1024)(128)(2,1)}, u32[]{:S(2)}) copy-start(bf16[4096]{0:T(1024)(128)(2,1)} %param.20) | copy-start | bytes 24580
  5.4 3.6 %copy-start.3 = (f32[32,8]{0,1:T(8,128)S(1)}, f32[32,8]{0,1:T(8,128)}, u32[]{:S(2)}) copy-start(f32[32,8]{0,1:T(8,128)} %param.22) | copy-start | bytes 3076
  5.4 3.6 %copy-start.5 = (s32[32,8]{0,1:T(8,128)S(1)}, s32[32,8]{0,1:T(8,128)}, u32[]{:S(2)}) copy-start(s32[32,8]{0,1:T(8,128)} %param.21) | copy-start | bytes 3076

commit v4 on v3

--- a/solution.py
+++ b/solution.py
@@ -194,30 +194,36 @@
                 device_id_type=pl.DeviceIdType.MESH,
             ).wait_recv()
 
-    def send_sum(slot, m, place, when=None):
+    half = block_rows // 2
+
+    def piece(ref, index, h):
+        return ref.at[index, h * half : (h + 1) * half]
+
+    def send_sum(slot, m, place, h, when=None):
         copy = pltpu.make_async_remote_copy(
-            src_ref=part.at[slot],
-            dst_ref=got.at[place],
+            src_ref=piece(part, slot, h),
+            dst_ref=piece(got, place, h),
             send_sem=send_sem.at[len(sent)],
-            recv_sem=sum_recv.at[place],
+            recv_sem=sum_recv.at[2 * place + h],
             device_id={"att": partners[m]},
             device_id_type=pl.DeviceIdType.MESH,
         )
         start(copy, when)
 
-    def sum_arrived(place):
+    def sum_arrived(place, h):
         pltpu.make_async_remote_copy(
-            src_ref=got.at[place],
-            dst_ref=got.at[place],
-            send_sem=sum_recv.at[place],
-            recv_sem=sum_recv.at[place],
+            src_ref=piece(got, place, h),
+            dst_ref=piece(got, place, h),
+            send_sem=sum_recv.at[2 * place + h],
+            recv_sem=sum_recv.at[2 * place + h],
             device_id={"att": partners[1]},
             device_id_type=pl.DeviceIdType.MESH,
         ).wait_recv()
 
-    def add(slot, place):
-        sum_arrived(place)
-        part[slot] = (part[slot].astype(jnp.float32) + got[place].astype(jnp.float32)).astype(
+    def add(slot, place, h):
+        sum_arrived(place, h)
+        held, came = piece(part, slot, h), piece(got, place, h)
+        held[...] = (held[...].astype(jnp.float32) + came[...].astype(jnp.float32)).astype(
             jnp.bfloat16
         )
 
@@ -247,13 +253,19 @@
             return carry
 
         lax.fori_loop(0, width // 512, out_step, 0)
-        for xr in (0, 1):
-            send_sum(first + 2 * xr + 1, 1, 2 * chunk + xr)
+        for xr in (1, 0):
+            for h in (0, 1):
+                send_sum(first + 2 * xr + 1, 1, 2 * chunk + xr, h)
 
     def across_x(chunk):
-        add(4 * chunk + 2, 2 * chunk + 1)
-        send_sum(4 * chunk + 2, 2, 8 + chunk)
-        add(4 * chunk, 2 * chunk)
+        for h in (0, 1):
+            add(4 * chunk + 2, 2 * chunk + 1, h)
+            send_sum(4 * chunk + 2, 2, 8 + chunk, h)
+        for h in (0, 1):
+            add(4 * chunk, 2 * chunk, h)
+
+    def inner_add(slot, place, h):
+        pl.when(inner_z)(functools.partial(add, slot, place, h))
 
     outer_z = jnp.logical_not(inner_z)
     forward(0, 2, 4)
@@ -292,24 +304,33 @@
     arrived(13, 15)
     experts(3)
     across_x(3)
+    for h in (0, 1):
+        add(8, 10, h)
+        send_sum(8, 4, 12, h, when=outer_z)
+    add(12, 11, 0)
+    send_sum(12, 4, 13, 0, when=outer_z)
     across_x(1)
-    add(8, 10)
-    send_sum(8, 4, 12, when=outer_z)
-    add(12, 11)
-    send_sum(12, 4, 13, when=outer_z)
+    add(12, 11, 1)
+    send_sum(12, 4, 13, 1, when=outer_z)
+    for h in (0, 1):
+        inner_add(12, 12, h)
+        send_sum(12, 12, 15, h, when=inner_z)
     across_x(0)
-    pl.when(inner_z)(functools.partial(add, 12, 12))
-    send_sum(12, 12, 15, when=inner_z)
-    pl.when(inner_z)(functools.partial(add, 8, 13))
-    send_sum(8, 12, 16, when=inner_z)
-    add(4, 9)
-    pl.when(inner_z)(functools.partial(add, 4, 16))
-    send_sum(4, 4, 14)
-    add(0, 8)
-    pl.when(inner_z)(functools.partial(add, 0, 15))
-    sum_arrived(14)
-    total = part[0].astype(jnp.float32) + got[14].astype(jnp.float32)
-    out_ref[...] = (hidden_ref[...].astype(jnp.float32) + total).astype(jnp.bfloat16)
+    for h in (0, 1):
+        inner_add(8, 13, h)
+        send_sum(8, 12, 16, h, when=inner_z)
+    for h in (0, 1):
+        add(4, 9, h)
+        inner_add(4, 16, h)
+        send_sum(4, 4, 14, h)
+    for h in (0, 1):
+        add(0, 8, h)
+        inner_add(0, 15, h)
+    for h in (0, 1):
+        sum_arrived(14, h)
+        span = slice(h * half, (h + 1) * half)
+        total = part[0, span].astype(jnp.float32) + got[14, span].astype(jnp.float32)
+        out_ref[span] = (hidden_ref[span].astype(jnp.float32) + total).astype(jnp.bfloat16)
     for copy, when in sent:
         if when is None:
             copy.wait_send()
@@ -362,9 +383,9 @@
             pltpu.VMEM((width, units), jnp.bfloat16),
             pltpu.VMEM((units, width), jnp.bfloat16),
             pltpu.SemaphoreType.DMA((3,)),
-            pltpu.SemaphoreType.DMA((40,)),
+            pltpu.SemaphoreType.DMA((64,)),
             pltpu.SemaphoreType.DMA((16,)),
-            pltpu.SemaphoreType.DMA((17,)),
+            pltpu.SemaphoreType.DMA((34,)),
         ],
         compiler_params=pltpu.CompilerParams(
             collective_id=0, has_side_effects=True, vmem_limit_bytes=48 * 1024 * 1024

time: 80.7 us -> 78.6 us (0.974)
  Pallas kernels: 70.5 us -> 68.4 us
    pallas_call x1, Pallas kernels: 70.5 us -> 68.4 us  [dense_body(): pl.pallas_call(expert_kernel, out_shape=jax.ShapeDtypeStruct((local_rows,...]
where the time goes in v4:
time: 78.6 us; the launch traced here: 78.4 us
  Pallas kernels  68.4 us (87%)
  matrix products  6.7 us (9%)
  local copies, waits for them, and re-layouts  2.03 us (3%)
  other arithmetic  1.15 us (1%)
    pallas_call x1, Pallas kernels, dense_body(): pl.pallas_call(expert_kernel, out_shape=jax.ShapeDtypeStruct((local_rows,...  68.4 us
    dot_general x1, matrix products, attend(): jnp.einsum('rghd,rgpd->rghp', query_blocks, key_cache, preferred_element_...  3.49 us
    dot_general x1, matrix products, attend(): jnp.einsum('rghp,rgpd->rghd', weights, value_cache, preferred_element_typ...  2.96 us
    unnamed x14, local copies, waits for them, and re-layouts  1.74 us

profile of v4, /device:TPU:0, one launch (start us, length us, event | category | flops | bytes accessed | tf_op | source)
XLA Modules:
  0.0 78.4 jit_solution(1570277928916561214)
XLA Ops:
  0.0 0.0 copy-start.1
  0.0 1.0 %copy.23 = bf16[4,8,32,128]{3,2,1,0:T(8,128)(2,1)S(1)} copy(bf16[4,8,32,128]{3,1,2,0:T(8,128)(2,1)} %bitcast.23) | data formatting | bytes 524288
  1.0 3.5 %fusion.13 = (f32[32,2,16]{2,1,0:T(2,128)S(1)}, f32[32,2,16,256]{3,2,1,0:T(8,128)S(1)}) fusion(bf16[32,2,16,128]{3,2,1,0:T(8,128)(2,1)S(1)} %bitcast.20, bf16[32,2,256,128]{3,2,1,0:T(8,128)(2,1)} %param.14, s32[32]{0:T(128)} %param.18), kind=kOutput, calls=%fused_computation.29 | convolution fusion | flops 68156416 | bytes 5509248 | tf_op jit(solution)/shard_map/rghd,rgpd->rghp/dot_general | solution.py:20
  4.5 0.0 copy-done.1
  4.5 0.2 fusion.14
  4.8 0.4 fusion.1
  5.3 0.0 copy-start
  5.3 0.1 fusion.10
  5.3 0.0 copy-done.2
  5.4 0.0 copy-start.4
  5.4 0.0 copy-start.3
  5.4 0.0 copy-start.5
  5.4 3.0 %convolution_add_fusion = f32[32,2,16,128]{3,2,1,0:T(8,128)S(1)} fusion(bf16[32,2,256,128]{3,2,1,0:T(8,128)(2,1)} %param.15, f32[32,2,16,256]{3,2,1,0:T(8,128)S(1)} %get-tuple-element.13, f32[32,2,16]{2,1,0:T(2,128)S(1)} %get-tuple-element.8, f32[32,2,16]{2,1,0:T(2,128)S(1)} %multiply_maximum_fusion, f32[32,2,128]{2,1,0:T(2,128)S(1)} %reshape.36, ...), kind=kOutput, calls=%fused_computation.2 | convolution fusion | flops 68157440 | bytes 5812224 | tf_op jit(solution)/shard_map/rghp,rgpd->rghd/dot_general | solution.py:38
  8.4 0.0 copy-done
  8.4 0.4 fusion.2
  8.8 0.0 copy-done.4
  8.8 0.1 fusion.4
  9.0 0.0 copy-done.3
  9.0 0.0 copy-done.5
  9.1 0.1 copy.18
  9.1 0.1 copy.19
  9.2 0.1 concatenate.3.block_ref
  9.3 68.4 %shard_map.127 = bf16[32,4096]{1,0:T(8,128)(2,1)S(1)} custom-call(bf16[32,4224]{1,0:T(8,128)(2,1)S(1)} %concatenate.3.block_ref, bf16[32,4096]{1,0:T(8,128)(2,1)S(1)} %get-tuple-element.6.hidden_ref, bf16[4096,768]{1,0:T(8,128)(2,1)} %bitcast.26, bf16[4096,768]{1,0:T(8,128)(2,1)} %bitcast.27, bf16[768,4096]{1,0:T(8,128)(2,1)} %bitcast.28), custom_call_target="tpu_custom_call" | custom-call | flops 9663676416 | bytes 18874368 | tf_op jit(solution)/shard_map/pallas_call | solution.py:372
  77.7 0.7 copy.28
  (12 shorter events, 0.1 us)
Async XLA Ops:
  0.0 4.5 %copy-start.1 = (bf16[32,256]{1,0:T(8,128)(2,1)S(1)}, bf16[32,256]{1,0:T(8,128)(2,1)}, u32[]{:S(2)}) copy-start(bf16[32,256]{1,0:T(8,128)(2,1)} %param.16) | copy-start | bytes 49156
  0.0 5.3 %copy-start.2 = (bf16[32,256]{1,0:T(8,128)(2,1)S(1)}, bf16[32,256]{1,0:T(8,128)(2,1)}, u32[]{:S(2)}) copy-start(bf16[32,256]{1,0:T(8,128)(2,1)} %param.17) | copy-start | bytes 49156
  5.3 3.1 %copy-start = (bf16[32,4096]{1,0:T(8,128)(2,1)S(1)}, bf16[32,4096]{1,0:T(8,128)(2,1)}, u32[]{:S(2)}) copy-start(bf16[32,4096]{1,0:T(8,128)(2,1)} %param.19) | copy-start | bytes 786436
  5.4 3.4 %copy-start.4 = (bf16[4096]{0:T(1024)(128)(2,1)S(1)}, bf16[4096]{0:T(1024)(128)(2,1)}, u32[]{:S(2)}) copy-start(bf16[4096]{0:T(1024)(128)(2,1)} %param.20) | copy-start | bytes 24580
  5.4 3.6 %copy-start.3 = (f32[32,8]{0,1:T(8,128)S(1)}, f32[32,8]{0,1:T(8,128)}, u32[]{:S(2)}) copy-start(f32[32,8]{0,1:T(8,128)} %param.22) | copy-start | bytes 3076
  5.4 3.6 %copy-start.5 = (s32[32,8]{0,1:T(8,128)S(1)}, s32[32,8]{0,1:T(8,128)}, u32[]{:S(2)}) copy-start(s32[32,8]{0,1:T(8,128)} %param.21) | copy-start | bytes 3076

commit v5 on v4

--- a/solution.py
+++ b/solution.py
@@ -298,9 +298,9 @@
     forward(10, 1)
     arrived(9, 11)
     experts(2)
-    across_x(2)
     arrived(14)
     forward(14, 1)
+    across_x(2)
     arrived(13, 15)
     experts(3)
     across_x(3)

time: 78.6 us -> 76.5 us (0.973)
  Pallas kernels: 68.4 us -> 66.3 us
    pallas_call x1, Pallas kernels: 68.4 us -> 66.3 us  [dense_body(): pl.pallas_call(expert_kernel, out_shape=jax.ShapeDtypeStruct((local_rows,...]
where the time goes in v5:
time: 76.5 us; the launch traced here: 76.3 us
  Pallas kernels  66.3 us (87%)
  matrix products  6.7 us (9%)
  local copies, waits for them, and re-layouts  2.03 us (3%)
  other arithmetic  1.15 us (2%)
    pallas_call x1, Pallas kernels, dense_body(): pl.pallas_call(expert_kernel, out_shape=jax.ShapeDtypeStruct((local_rows,...  66.3 us
    dot_general x1, matrix products, attend(): jnp.einsum('rghd,rgpd->rghp', query_blocks, key_cache, preferred_element_...  3.49 us
    dot_general x1, matrix products, attend(): jnp.einsum('rghp,rgpd->rghd', weights, value_cache, preferred_element_typ...  2.96 us
    unnamed x14, local copies, waits for them, and re-layouts  1.74 us

profile of v5, /device:TPU:0, one launch (start us, length us, event | category | flops | bytes accessed | tf_op | source)
XLA Modules:
  0.0 76.3 jit_solution(9172263562668080064)
XLA Ops:
  0.0 0.0 copy-start.1
  0.0 1.0 %copy.23 = bf16[4,8,32,128]{3,2,1,0:T(8,128)(2,1)S(1)} copy(bf16[4,8,32,128]{3,1,2,0:T(8,128)(2,1)} %bitcast.23) | data formatting | bytes 524288
  1.0 3.5 %fusion.13 = (f32[32,2,16]{2,1,0:T(2,128)S(1)}, f32[32,2,16,256]{3,2,1,0:T(8,128)S(1)}) fusion(bf16[32,2,16,128]{3,2,1,0:T(8,128)(2,1)S(1)} %bitcast.20, bf16[32,2,256,128]{3,2,1,0:T(8,128)(2,1)} %param.14, s32[32]{0:T(128)} %param.18), kind=kOutput, calls=%fused_computation.29 | convolution fusion | flops 68156416 | bytes 5509248 | tf_op jit(solution)/shard_map/rghd,rgpd->rghp/dot_general | solution.py:20
  4.5 0.0 copy-done.1
  4.5 0.2 fusion.14
  4.8 0.4 fusion.1
  5.3 0.0 copy-start
  5.3 0.1 fusion.10
  5.3 0.0 copy-done.2
  5.4 0.0 copy-start.4
  5.4 0.0 copy-start.3
  5.4 0.0 copy-start.5
  5.4 3.0 %convolution_add_fusion = f32[32,2,16,128]{3,2,1,0:T(8,128)S(1)} fusion(bf16[32,2,256,128]{3,2,1,0:T(8,128)(2,1)} %param.15, f32[32,2,16,256]{3,2,1,0:T(8,128)S(1)} %get-tuple-element.13, f32[32,2,16]{2,1,0:T(2,128)S(1)} %get-tuple-element.8, f32[32,2,16]{2,1,0:T(2,128)S(1)} %multiply_maximum_fusion, f32[32,2,128]{2,1,0:T(2,128)S(1)} %reshape.36, ...), kind=kOutput, calls=%fused_computation.2 | convolution fusion | flops 68157440 | bytes 5812224 | tf_op jit(solution)/shard_map/rghp,rgpd->rghd/dot_general | solution.py:38
  8.4 0.0 copy-done
  8.4 0.4 fusion.2
  8.8 0.0 copy-done.4
  8.8 0.1 fusion.4
  9.0 0.0 copy-done.3
  9.0 0.0 copy-done.5
  9.1 0.1 copy.18
  9.1 0.1 copy.19
  9.2 0.1 concatenate.3.block_ref
  9.3 66.3 %shard_map.127 = bf16[32,4096]{1,0:T(8,128)(2,1)S(1)} custom-call(bf16[32,4224]{1,0:T(8,128)(2,1)S(1)} %concatenate.3.block_ref, bf16[32,4096]{1,0:T(8,128)(2,1)S(1)} %get-tuple-element.6.hidden_ref, bf16[4096,768]{1,0:T(8,128)(2,1)} %bitcast.26, bf16[4096,768]{1,0:T(8,128)(2,1)} %bitcast.27, bf16[768,4096]{1,0:T(8,128)(2,1)} %bitcast.28), custom_call_target="tpu_custom_call" | custom-call | flops 9663676416 | bytes 18874368 | tf_op jit(solution)/shard_map/pallas_call | solution.py:372
  75.6 0.7 copy.28
  (12 shorter events, 0.1 us)
Async XLA Ops:
  0.0 4.5 %copy-start.1 = (bf16[32,256]{1,0:T(8,128)(2,1)S(1)}, bf16[32,256]{1,0:T(8,128)(2,1)}, u32[]{:S(2)}) copy-start(bf16[32,256]{1,0:T(8,128)(2,1)} %param.16) | copy-start | bytes 49156
  0.0 5.3 %copy-start.2 = (bf16[32,256]{1,0:T(8,128)(2,1)S(1)}, bf16[32,256]{1,0:T(8,128)(2,1)}, u32[]{:S(2)}) copy-start(bf16[32,256]{1,0:T(8,128)(2,1)} %param.17) | copy-start | bytes 49156
  5.3 3.1 %copy-start = (bf16[32,4096]{1,0:T(8,128)(2,1)S(1)}, bf16[32,4096]{1,0:T(8,128)(2,1)}, u32[]{:S(2)}) copy-start(bf16[32,4096]{1,0:T(8,128)(2,1)} %param.19) | copy-start | bytes 786436
  5.4 3.4 %copy-start.4 = (bf16[4096]{0:T(1024)(128)(2,1)S(1)}, bf16[4096]{0:T(1024)(128)(2,1)}, u32[]{:S(2)}) copy-start(bf16[4096]{0:T(1024)(128)(2,1)} %param.20) | copy-start | bytes 24580
  5.4 3.6 %copy-start.3 = (f32[32,8]{0,1:T(8,128)S(1)}, f32[32,8]{0,1:T(8,128)}, u32[]{:S(2)}) copy-start(f32[32,8]{0,1:T(8,128)} %param.22) | copy-start | bytes 3076
  5.4 3.6 %copy-start.5 = (s32[32,8]{0,1:T(8,128)S(1)}, s32[32,8]{0,1:T(8,128)}, u32[]{:S(2)}) copy-start(s32[32,8]{0,1:T(8,128)} %param.21) | copy-start | bytes 3076
